TPU v7x, 256 devices: a whole 4x4x8 slice. The times are simulated.
256 devices in a mesh: dp: 32 (over y, z_lo, core), pos: 8 (over z_hi, x).
Axes of the slice: x: 4, y: 4, z: 8 (z_hi: 2, z_lo: 4; z = z_hi * 4 + z_lo), core: 2. Of those that a mesh axis runs over, the one named last changes fastest.
Arguments:
- inputs: bfloat16 [64, 2048, 512], P('dp', 'pos'), may hold values from -6 to 6
- pre_act: bfloat16 [64, 2048, 512], P('dp', 'pos'), may hold values from -6 to 6
- grad_out: bfloat16 [64, 2048, 512], P('dp', 'pos'), may hold values from -6 to 6
- weight: bfloat16 [512, 9, 512], P(('dp', 'pos')), may hold values from -0.09375 to 0.09375
Outputs:
- grad_input: bfloat16 [64, 2048, 512], P('dp', 'pos')
- grad_weight: float32 [512, 9, 512], P(('dp', 'pos'))
All inputs are finite; a program needn't handle non-finite values.
Results may differ from a plain program's by a relative error of at most 0.005.
Values may be sent and summed in bfloat16 or wider, within the bound.
A program may use at most 128 MiB of HBM per device.

v0:
```python
import jax
import jax.numpy as jnp
from jax import lax
from jax.sharding import PartitionSpec as P

K = 9


def padded_2(block, sides, width):
    for axis, dim in sides:
        count = lax.axis_size(axis)
        forward = [(i, i + 1) for i in range(count - 1)]
        backward = [(target, source) for source, target in forward]
        low = lax.ppermute(
            lax.slice_in_dim(block, block.shape[dim] - width, None, axis=dim), axis, forward
        )
        high = lax.ppermute(lax.slice_in_dim(block, 0, width, axis=dim), axis, backward)
        block = jnp.concatenate([low, block, high], axis=dim)
    return block


def partner(block, axis, distance):
    count = lax.axis_size(axis)
    route = []
    for low in range(count):
        high = low | 1 << distance
        if high != low and high < count:
            route += [(low, high), (high, low)]
    return lax.ppermute(block, axis, route)


def gelu_slope(values):
    cdf = 0.5 * (1.0 + lax.erf(values * 0.7071067811865476))
    return cdf + values * jnp.exp(-0.5 * values * values) * 0.3989422804014327


def on_device(inputs, pre_act, grad_out, weight):
    seq_count, length, chan_width = inputs.shape
    half_width = (K - 1) // 2
    grad_pre = (grad_out.astype(jnp.float32) * gelu_slope(pre_act.astype(jnp.float32))).astype(
        jnp.bfloat16
    )
    stacked = jnp.stack([inputs, grad_pre])
    padded = padded_2(stacked, (("pos", 2),), half_width)
    whole = lax.all_gather(weight, ("dp", "pos"), axis=0, tiled=True)
    bit_count = lax.axis_size("pos").bit_length() - 1
    mirrored = padded
    for bit_num in range(bit_count):
        mirrored = partner(mirrored, "pos", bit_num)
    reverse = jnp.flip(mirrored, axis=(2, 3))
    both_inputs = jnp.stack([padded[0], reverse[0]])
    both_grads = jnp.stack([padded[1], reverse[1]])
    total = jnp.zeros((2, seq_count, length, chan_width), jnp.float32)
    for offset in range(K):
        begin = K - 1 - offset
        total = total + jnp.einsum(
            "bsto,io->bsti",
            both_grads[:, :, begin : begin + length],
            whole[:, offset, :],
            preferred_element_type=jnp.float32,
        )
    returned = total[1]
    for bit_num in range(bit_count):
        returned = partner(returned, "pos", bit_num)
    grad_input = (total[0] + jnp.flip(returned, axis=(1, 2))).astype(jnp.bfloat16)
    centre_grads = both_grads[:, :, half_width : half_width + length]
    full_terms = jnp.stack(
        [
            jnp.einsum(
                "bsti,bsto->io",
                both_inputs[:, :, offset : offset + length],
                centre_grads,
                preferred_element_type=jnp.float32,
            )
            for offset in range(K)
        ],
        axis=1,
    )
    grad_weight = lax.psum_scatter(full_terms, ("dp", "pos"), scatter_dimension=0, tiled=True)
    return (grad_input, grad_weight)


def solution(mesh):
    placed = (
        P("dp", "pos", None),
        P("dp", "pos", None),
        P("dp", "pos", None),
        P(("dp", "pos"), None, None),
    )
    return jax.shard_map(
        on_device,
        mesh=mesh,
        in_specs=placed,
        out_specs=(P("dp", "pos", None), P(("dp", "pos"), None, None)),
        check_vma=False,
    )
```

profile of v0, /device:TPU:97, one launch (start us, length us, event | category | flops | bytes accessed | tf_op | source)
XLA Modules:
  0.0 1133.1 jit_solution(16518667106808815034)
XLA Ops:
  7.2 0.0 copy-start
  7.2 0.0 all-gather.2.cloned.1.call-start
  7.2 1.4 copy.15
  8.6 0.0 all-gather.2.cloned.1.call-update
  8.6 0.0 all-reduce.3.cloned.1.call-start
  8.7 1.7 fusion.60
  10.4 0.8 pad_maximum_fusion.6
  11.1 3.1 collective-permute-start
  14.3 1.3 collective-permute-start.1
  15.6 0.0 collective-permute-done
  15.6 3.2 collective-permute-done.1
  18.8 0.0 copy-done
  18.8 0.3 pad_maximum_fusion
  19.0 1.3 collective-permute-start.2
  20.3 22.0 %collective-permute-done.2 = bf16[2,2,264,512]{3,2,1,0:T(8,128)(2,1)S(1)} collective-permute-done((bf16[2,2,264,512]{3,2,1,0:T(8,128)(2,1)S(1)}, bf16[2,2,264,512]{3,2,1,0:T(8,128)(2,1)S(1)}, u32[]{:S(2)}, u32[]{:S(2)}) %collective-permute-start.2) | collective-permute-done | bytes 1081376 | tf_op jit(solution)/shard_map/ppermute | solution.py:29
  42.4 13.7 %collective-permute-start.3 = (bf16[2,2,264,512]{3,2,1,0:T(8,128)(2,1)S(1)}, bf16[2,2,264,512]{3,2,1,0:T(8,128)(2,1)S(1)}, u32[]{:S(2)}, u32[]{:S(2)}) collective-permute-start(bf16[2,2,264,512]{3,2,1,0:T(8,128)(2,1)S(1)} %collective-permute-done.2), channel_id=1, source_target_pairs={{0,2},{2,0},{1,3},{3,1},{4,6},{6,4},{5,7},{7,5},{8,10},{10,8},{9,1... | collective-permute-start | bytes 3244040 | tf_op jit(solution)/shard_map/ppermute | solution.py:29
  56.1 23.8 %collective-permute-done.3 = bf16[2,2,264,512]{3,2,1,0:T(8,128)(2,1)S(1)} collective-permute-done((bf16[2,2,264,512]{3,2,1,0:T(8,128)(2,1)S(1)}, bf16[2,2,264,512]{3,2,1,0:T(8,128)(2,1)S(1)}, u32[]{:S(2)}, u32[]{:S(2)}) %collective-permute-start.3) | collective-permute-done | bytes 1081376 | tf_op jit(solution)/shard_map/ppermute | solution.py:29
  79.9 0.0 collective-permute-start.4
  79.9 0.1 fusion.80
  80.0 34.6 %collective-permute-done.4 = bf16[2,2,264,512]{3,2,1,0:T(8,128)(2,1)S(1)} collective-permute-done((bf16[2,2,264,512]{3,2,1,0:T(8,128)(2,1)S(1)}, bf16[2,2,264,512]{3,2,1,0:T(8,128)(2,1)S(1)}, u32[]{:S(2)}, u32[]{:S(2)}) %collective-permute-start.4) | collective-permute-done | bytes 1081376 | tf_op jit(solution)/shard_map/ppermute | solution.py:29
  114.6 0.1 fusion.79
  114.7 3.1 slice.116
  117.8 3.1 slice.139
  121.0 0.3 fusion.47
  121.3 1.7 fusion.8
  123.0 1.7 fusion.7
  124.8 1.8 fusion.6
  126.6 1.8 fusion.5
  128.4 1.7 fusion.4
  130.1 1.7 fusion.3
  131.8 1.8 fusion.2
  133.6 1.7 fusion.1
  135.3 1.7 fusion
  137.1 0.0 all-reduce.3.cloned.1.call-update
  137.1 619.3 %all-gather.2.cloned.1.call-done = bf16[512,9,512]{2,1,0:T(8,128)(2,1)} async-done(((bf16[2,9,512]{2,1,0:T(8,128)(2,1)}), bf16[512,9,512]{2,1,0:T(8,128)(2,1)}) %all-gather.2.cloned.1.call-update) | async-done | bytes 4718608 | tf_op jit(solution)/shard_map/all_gather | solution.py:45
  756.4 19.3 %fusion.78 = (bf16[512,1,512]{2,1,0:T(2,128)(2,1)S(1)}, bf16[512,1,512]{2,1,0:T(2,128)(2,1)S(1)}, bf16[512,1,512]{2,1,0:T(2,128)(2,1)S(1)}, bf16[512,1,512]{2,1,...) fusion(bf16[512,9,512]{2,1,0:T(8,128)(2,1)} %all-gather.2.clone, ...), kind=kLoop, calls=%fused_computation.126 | loop fusion | bytes 9437184 | tf_op jit(solution)/shard_map/slice | solution.py:59
  775.8 0.7 fusion.36
  776.5 0.8 fusion.39
  777.3 0.8 fusion.42
  778.0 0.7 fusion.45
  778.8 0.8 fusion.49
  779.5 0.8 fusion.52
  780.3 0.8 fusion.33
  781.1 0.7 fusion.59
  781.8 1.6 add_add_fusion
  783.4 0.1 slice_bitcast_fusion
  783.5 37.9 %collective-permute-start.5 = (f32[2,256,512]{2,1,0:T(8,128)S(1)}, f32[2,256,512]{2,1,0:T(8,128)S(1)}, u32[]{:S(2)}, u32[]{:S(2)}) collective-permute-start(f32[2,256,512]{2,1,0:T(8,128)S(1)} %slice_bitcast_fusion), channel_id=1, source_target_pairs={{0,1},{1,0},{2,3},{3,2},{4,5},{5,4},{6,7},{7,6},{8,9},{9,8},{10,11... | collective-permute-start | bytes 3145736 | tf_op jit(solution)/shard_map/ppermute | solution.py:29
  821.4 25.9 %collective-permute-done.5 = f32[2,256,512]{2,1,0:T(8,128)S(1)} collective-permute-done((f32[2,256,512]{2,1,0:T(8,128)S(1)}, f32[2,256,512]{2,1,0:T(8,128)S(1)}, u32[]{:S(2)}, u32[]{:S(2)}) %collective-permute-start.5) | collective-permute-done | bytes 1048608 | tf_op jit(solution)/shard_map/ppermute | solution.py:29
  847.3 1.3 collective-permute-start.6
  848.5 24.0 %collective-permute-done.6 = f32[2,256,512]{2,1,0:T(8,128)S(1)} collective-permute-done((f32[2,256,512]{2,1,0:T(8,128)S(1)}, f32[2,256,512]{2,1,0:T(8,128)S(1)}, u32[]{:S(2)}, u32[]{:S(2)}) %collective-permute-start.6) | collective-permute-done | bytes 1048608 | tf_op jit(solution)/shard_map/ppermute | solution.py:29
  872.5 0.0 collective-permute-start.7
  872.5 243.8 %all-reduce.3.cloned.1.call-done = f32[512,9,512]{2,0,1:T(8,128)} async-done(((f32[512,9,512]{2,0,1:T(8,128)}), f32[512,9,512]{2,0,1:T(8,128)}) %all-reduce.3.cloned.1.call-update) | async-done | bytes 9437200
  1116.3 1.5 constant_dynamic-slice_fusion
  1117.8 0.0 collective-permute-done.7
  1117.8 7.5 rev.6
  1125.3 1.0 fusion.56
Async XLA Ops:
  7.2 11.6 %copy-start = (bf16[2,256,512]{2,1,0:T(8,128)(2,1)S(1)}, bf16[2,256,512]{2,1,0:T(8,128)(2,1)}, u32[]{:S(2)}) copy-start(bf16[2,256,512]{2,1,0:T(8,128)(2,1)} %param.4) | copy-start | bytes 1572868
  7.2 749.3 %all-gather.2.cloned.1.call-start = ((), (), s32[]{:S(2)}) async-start(), calls=%async_computation | async-start | bytes 8421376 | tf_op jit(solution)/shard_map/all_gather | solution.py:45
  8.6 1107.7 %all-reduce.3.cloned.1.call-start = ((), (), s32[]{:S(2)}) async-start(), calls=%async_computation.1 | async-start | bytes 18874368
  11.1 4.4 collective-permute-start
  14.3 4.5 collective-permute-start.1
  19.0 23.3 %collective-permute-start.2 = (bf16[2,2,264,512]{3,2,1,0:T(8,128)(2,1)S(1)}, bf16[2,2,264,512]{3,2,1,0:T(8,128)(2,1)S(1)}, u32[]{:S(2)}, u32[]{:S(2)}) collective-permute-start(bf16[2,2,264,512]{3,2,1,0:T(8,128)(2,1)S(1)} %pad_maximum_fusion), channel_id=1, source_target_pairs={{0,1},{1,0},{2,3},{3,2},{4,5},{5,4},{6,7},{7,6},{8,9},{9,8},{10,11... | collective-permute-start | bytes 3244040 | tf_op jit(solution)/shard_map/ppermute | solution.py:29
  42.4 37.5 %collective-permute-start.3 = (bf16[2,2,264,512]{3,2,1,0:T(8,128)(2,1)S(1)}, bf16[2,2,264,512]{3,2,1,0:T(8,128)(2,1)S(1)}, u32[]{:S(2)}, u32[]{:S(2)}) collective-permute-start(bf16[2,2,264,512]{3,2,1,0:T(8,128)(2,1)S(1)} %collective-permute-done.2), channel_id=1, source_target_pairs={{0,2},{2,0},{1,3},{3,1},{4,6},{6,4},{5,7},{7,5},{8,10},{10,8},{9,1... | collective-permute-start | bytes 3244040 | tf_op jit(solution)/shard_map/ppermute | solution.py:29
  79.9 34.7 %collective-permute-start.4 = (bf16[2,2,264,512]{3,2,1,0:T(8,128)(2,1)S(1)}, bf16[2,2,264,512]{3,2,1,0:T(8,128)(2,1)S(1)}, u32[]{:S(2)}, u32[]{:S(2)}) collective-permute-start(bf16[2,2,264,512]{3,2,1,0:T(8,128)(2,1)S(1)} %collective-permute-done.3), channel_id=1, source_target_pairs={{0,4},{4,0},{1,5},{5,1},{2,6},{6,2},{3,7},{7,3},{8,12},{12,8},{9,1... | collective-permute-start | bytes 3244040 | tf_op jit(solution)/shard_map/ppermute | solution.py:29
  783.5 63.8 %collective-permute-start.5 = (f32[2,256,512]{2,1,0:T(8,128)S(1)}, f32[2,256,512]{2,1,0:T(8,128)S(1)}, u32[]{:S(2)}, u32[]{:S(2)}) collective-permute-start(f32[2,256,512]{2,1,0:T(8,128)S(1)} %slice_bitcast_fusion), channel_id=1, source_target_pairs={{0,1},{1,0},{2,3},{3,2},{4,5},{5,4},{6,7},{7,6},{8,9},{9,8},{10,11... | collective-permute-start | bytes 3145736 | tf_op jit(solution)/shard_map/ppermute | solution.py:29
  847.3 25.2 %collective-permute-start.6 = (f32[2,256,512]{2,1,0:T(8,128)S(1)}, f32[2,256,512]{2,1,0:T(8,128)S(1)}, u32[]{:S(2)}, u32[]{:S(2)}) collective-permute-start(f32[2,256,512]{2,1,0:T(8,128)S(1)} %collective-permute-done.5), channel_id=1, source_target_pairs={{0,2},{2,0},{1,3},{3,1},{4,6},{6,4},{5,7},{7,5},{8,10},{10,8},{9,1... | collective-permute-start | bytes 3145736 | tf_op jit(solution)/shard_map/ppermute | solution.py:29
  872.5 245.3 %collective-permute-start.7 = (f32[2,256,512]{2,1,0:T(8,128)S(1)}, f32[2,256,512]{2,1,0:T(8,128)}, u32[]{:S(2)}, u32[]{:S(2)}) collective-permute-start(f32[2,256,512]{2,1,0:T(8,128)S(1)} %collective-permute-done.6), channel_id=1, source_target_pairs={{0,4},{4,0},{1,5},{5,1},{2,6},{6,2},{3,7},{7,3},{8,12},{12,8},{9,1... | collective-permute-start | bytes 3145736 | tf_op jit(solution)/shard_map/ppermute | solution.py:29
Sparse Core Ops, SparseCore 0:
  10.5 745.9 all-gather.1
  762.0 354.2 all-reduce.2
where the time goes:
time: 1130 us
  waiting for transfers between devices  997 us (88%)
  starting transfers between devices  58.7 us (5%)
  local copies, waits for them, and re-layouts  36.3 us (3%)
  matrix products  23.3 us (2%)
  between operations  14.2 us (1%)
    all_gather x1, waiting for transfers between devices, on_device(): whole = lax.all_gather(weight, ('dp', 'pos'), axis=0, tiled=True)  619 us
    unnamed x3, waiting for transfers between devices  244 us
    ppermute x6, waiting for transfers between devices, partner(): return lax.ppermute(block, axis, route)  130 us
    ppermute x6, starting transfers between devices, partner(): return lax.ppermute(block, axis, route)  54.2 us
  transfers between devices with their start and end apart: 10, of which 8 were waited for; matrix products, arithmetic and copies ran while one was open for 5% of the time, Pallas kernels for 0%

commit v1 on v0

--- a/solution.py
+++ b/solution.py
@@ -42,7 +42,8 @@
     )
     stacked = jnp.stack([inputs, grad_pre])
     padded = padded_2(stacked, (("pos", 2),), half_width)
-    whole = lax.all_gather(weight, ("dp", "pos"), axis=0, tiled=True)
+    outgoing = jnp.stack([weight] * lax.axis_size(("dp", "pos")))
+    whole = jnp.concatenate(lax.all_to_all(outgoing, ("dp", "pos"), 0, 0), axis=0)
     bit_count = lax.axis_size("pos").bit_length() - 1
     mirrored = padded
     for bit_num in range(bit_count):

time: 1130 us -> 613 us (0.54)
  waiting for transfers between devices: 997 us -> 438 us
  starting transfers between devices: 58.7 us -> 94.9 us
    all_gather x1 -> x0, waiting for transfers between devices: 619 us -> none  [on_device(): whole = lax.all_gather(weight, ('dp', 'pos'), axis=0, tiled=True)]
    unnamed x3 -> x2, waiting for transfers between devices: 244 us -> 278 us
    ppermute x6, waiting for transfers between devices: 130 us -> 153 us  [partner(): return lax.ppermute(block, axis, route)]
    ppermute x6, starting transfers between devices: 54.2 us -> 75.3 us  [partner(): return lax.ppermute(block, axis, route)]
    slice x1 -> x0, local copies, waits for them, and re-layouts: 19.3 us -> none  [on_device(): whole[:, offset, :]]
    all_to_all x0 -> x1, starting transfers between devices: none -> 15.2 us  [on_device(): lax.all_to_all(outgoing, ('dp', 'pos'), 0, 0)]
  transfers between devices with their start and end apart: 10 -> 10, of which waited for: 8 -> 8; matrix products, arithmetic and copies ran while one was open for 5% -> 8% of each run, Pallas kernels for 0% -> 0%
where the time goes in v1:
time: 613 us; the launch traced here: 612 us
  waiting for transfers between devices  438 us (71%)
  starting transfers between devices  94.9 us (15%)
  local copies, waits for them, and re-layouts  37.2 us (6%)
  matrix products  25.2 us (4%)
  between operations  14.2 us (2%)
    unnamed x2, waiting for transfers between devices  278 us
    ppermute x6, waiting for transfers between devices, partner(): return lax.ppermute(block, axis, route)  153 us
    ppermute x6, starting transfers between devices, partner(): return lax.ppermute(block, axis, route)  75.3 us
    dot_general x9, matrix products, on_device(): jnp.einsum('bsti,bsto->io', both_inputs[:, :, offset:offset + length], ce...  15.8 us
    all_to_all x1, starting transfers between devices, on_device(): lax.all_to_all(outgoing, ('dp', 'pos'), 0, 0)  15.2 us
  transfers between devices with their start and end apart: 10, of which 8 were waited for; matrix products, arithmetic and copies ran while one was open for 8% of the time, Pallas kernels for 0%

profile of v1, /device:TPU:97, one launch (start us, length us, event | category | flops | bytes accessed | tf_op | source)
XLA Modules:
  0.0 611.8 jit_solution(17168105684709080449)
XLA Ops:
  7.2 5.4 stack.36
  12.5 0.0 copy-start.2
  12.5 0.0 copy-start.3
  12.5 0.0 copy-start.1
  12.5 15.2 %all-to-all-start = ((bf16[256,2,9,512]{3,1,2,0:T(2,128)(2,1)}), bf16[256,2,9,512]{3,1,2,0:T(2,128)(2,1)}, u32[]{:S(2)}, u32[]{:S(2)}) async-start(bf16[256,2,9,512]{3,1,2,0:T(2,128)(2,1)} %stack.36), calls=%async_computation | async-start | bytes 9437184 | tf_op jit(solution)/shard_map/all_to_all | solution.py:46
  27.8 0.0 all-reduce.3.cloned.1.call-start
  27.8 0.0 copy-done.2
  27.8 0.0 copy-done.3
  27.8 0.5 fusion.60
  28.3 0.0 copy-done.1
  28.4 3.1 collective-permute-start
  31.5 1.3 collective-permute-start.1
  32.8 2.5 collective-permute-done
  35.3 4.2 collective-permute-done.1
  39.5 0.3 pad_maximum_fusion
  39.8 0.1 collective-permute-start.2
  39.9 44.0 %collective-permute-done.2 = bf16[2,2,264,512]{3,2,1,0:T(8,128)(2,1)S(1)} collective-permute-done((bf16[2,2,264,512]{3,2,1,0:T(8,128)(2,1)S(1)}, bf16[2,2,264,512]{3,2,1,0:T(8,128)(2,1)S(1)}, u32[]{:S(2)}, u32[]{:S(2)}) %collective-permute-start.2) | collective-permute-done | bytes 1081376 | tf_op jit(solution)/shard_map/ppermute | solution.py:29
  83.8 74.0 %collective-permute-start.3 = (bf16[2,2,264,512]{3,2,1,0:T(8,128)(2,1)S(1)}, bf16[2,2,264,512]{3,2,1,0:T(8,128)(2,1)S(1)}, u32[]{:S(2)}, u32[]{:S(2)}) collective-permute-start(bf16[2,2,264,512]{3,2,1,0:T(8,128)(2,1)S(1)} %collective-permute-done.2), channel_id=1, source_target_pairs={{0,2},{2,0},{1,3},{3,1},{4,6},{6,4},{5,7},{7,5},{8,10},{10,8},{9,1... | collective-permute-start | bytes 3244040 | tf_op jit(solution)/shard_map/ppermute | solution.py:29
  157.8 23.1 %collective-permute-done.3 = bf16[2,2,264,512]{3,2,1,0:T(8,128)(2,1)S(1)} collective-permute-done((bf16[2,2,264,512]{3,2,1,0:T(8,128)(2,1)S(1)}, bf16[2,2,264,512]{3,2,1,0:T(8,128)(2,1)S(1)}, u32[]{:S(2)}, u32[]{:S(2)}) %collective-permute-start.3) | collective-permute-done | bytes 1081376 | tf_op jit(solution)/shard_map/ppermute | solution.py:29
  180.9 0.6 collective-permute-start.4
  181.5 0.1 fusion.79
  181.5 27.2 %collective-permute-done.4 = bf16[2,2,264,512]{3,2,1,0:T(8,128)(2,1)S(1)} collective-permute-done((bf16[2,2,264,512]{3,2,1,0:T(8,128)(2,1)S(1)}, bf16[2,2,264,512]{3,2,1,0:T(8,128)(2,1)S(1)}, u32[]{:S(2)}, u32[]{:S(2)}) %collective-permute-start.4) | collective-permute-done | bytes 1081376 | tf_op jit(solution)/shard_map/ppermute | solution.py:29
  208.7 0.1 fusion.78
  208.8 3.1 slice.116
  212.0 3.1 slice.139
  215.1 0.3 fusion.47
  215.5 1.7 fusion.8
  217.2 1.7 fusion.7
  218.9 1.8 fusion.6
  220.7 1.8 fusion.5
  222.5 1.7 fusion.4
  224.2 1.8 fusion.3
  226.0 1.8 fusion.2
  227.7 1.8 fusion.1
  229.5 1.7 fusion
  231.2 0.0 all-reduce.3.cloned.1.call-update
  231.2 0.0 all-to-all-done
  231.3 8.3 %copy.15 = bf16[256,2,9,512]{3,1,0,2:T(2,128)(2,1)} copy(bf16[256,2,9,512]{3,1,2,0:T(2,128)(2,1)} %all-to-all-done) | data formatting | bytes 9437184 | tf_op jit(solution)/shard_map/all_to_all | solution.py:46
  239.5 8.1 %reshape.9 = bf16[512,9,512]{2,0,1:T(8,128)(2,1)} reshape(bf16[256,2,9,512]{3,1,0,2:T(2,128)(2,1)} %copy.15) | data formatting | bytes 9437184 | tf_op jit(solution)/shard_map/reshape | solution.py:46
  247.6 0.0 copy-start
  247.6 1.9 fusion.36
  249.5 1.8 fusion.39
  251.3 0.0 copy-done
  251.3 0.7 fusion.42
  252.1 0.7 fusion.45
  252.8 0.8 fusion.49
  253.6 0.7 fusion.52
  254.3 0.7 fusion.33
  255.1 0.7 fusion.59
  255.8 1.2 add_add_fusion
  257.0 0.1 slice_bitcast_fusion
  257.1 0.6 collective-permute-start.5
  257.8 26.2 %collective-permute-done.5 = f32[2,256,512]{2,1,0:T(8,128)S(1)} collective-permute-done((f32[2,256,512]{2,1,0:T(8,128)S(1)}, f32[2,256,512]{2,1,0:T(8,128)S(1)}, u32[]{:S(2)}, u32[]{:S(2)}) %collective-permute-start.5) | collective-permute-done | bytes 1048608 | tf_op jit(solution)/shard_map/ppermute | solution.py:29
  284.0 0.0 collective-permute-start.6
  284.0 32.5 %collective-permute-done.6 = f32[2,256,512]{2,1,0:T(8,128)S(1)} collective-permute-done((f32[2,256,512]{2,1,0:T(8,128)S(1)}, f32[2,256,512]{2,1,0:T(8,128)S(1)}, u32[]{:S(2)}, u32[]{:S(2)}) %collective-permute-start.6) | collective-permute-done | bytes 1048608 | tf_op jit(solution)/shard_map/ppermute | solution.py:29
  316.5 0.0 collective-permute-start.7
  316.5 278.4 %all-reduce.3.cloned.1.call-done = f32[512,9,512]{2,0,1:T(8,128)} async-done(((f32[512,9,512]{2,0,1:T(8,128)}), f32[512,9,512]{2,0,1:T(8,128)}) %all-reduce.3.cloned.1.call-update) | async-done | bytes 9437200
  595.0 1.5 constant_dynamic-slice_fusion
  596.5 0.0 collective-permute-done.7
  596.5 7.5 %rev.6 = f32[2,256,512]{2,1,0:T(8,128)S(1)} reverse(f32[2,256,512]{2,1,0:T(8,128)} %collective-permute-done.7), dimensions={1,2} | reverse | bytes 2097152 | tf_op jit(solution)/shard_map/jit(_flip)/rev | solution.py:66
  604.0 1.0 fusion.56
  (1 shorter events, 0.0 us)
Async XLA Ops:
  12.5 15.3 %copy-start.2 = (bf16[2,256,512]{2,1,0:T(8,128)(2,1)S(1)}, bf16[2,256,512]{2,1,0:T(8,128)(2,1)}, u32[]{:S(2)}) copy-start(bf16[2,256,512]{2,1,0:T(8,128)(2,1)} %param.5) | copy-start | bytes 1572868
  12.5 15.3 %copy-start.3 = (bf16[2,256,512]{2,1,0:T(8,128)(2,1)S(1)}, bf16[2,256,512]{2,1,0:T(8,128)(2,1)}, u32[]{:S(2)}) copy-start(bf16[2,256,512]{2,1,0:T(8,128)(2,1)} %param.6) | copy-start | bytes 1572868
  12.5 15.8 %copy-start.1 = (bf16[2,256,512]{2,1,0:T(8,128)(2,1)S(1)}, bf16[2,256,512]{2,1,0:T(8,128)(2,1)}, u32[]{:S(2)}) copy-start(bf16[2,256,512]{2,1,0:T(8,128)(2,1)} %param.4) | copy-start | bytes 1572868
  12.5 218.7 %all-to-all-start = ((bf16[256,2,9,512]{3,1,2,0:T(2,128)(2,1)}), bf16[256,2,9,512]{3,1,2,0:T(2,128)(2,1)}, u32[]{:S(2)}, u32[]{:S(2)}) async-start(bf16[256,2,9,512]{3,1,2,0:T(2,128)(2,1)} %stack.36), calls=%async_computation | async-start | bytes 9437184 | tf_op jit(solution)/shard_map/all_to_all | solution.py:46
  27.8 567.2 %all-reduce.3.cloned.1.call-start = ((), (), s32[]{:S(2)}) async-start(), calls=%async_computation.1 | async-start | bytes 18874368
  28.4 6.9 %collective-permute-start = (bf16[2,2,4,512]{3,2,1,0:T(4,128)(2,1)S(1)}, bf16[2,2,4,512]{3,2,1,0:T(4,128)(2,1)S(1)}, u32[]{:S(2)}, u32[]{:S(2)}) collective-permute-start(bf16[2,2,4,512]{3,2,1,0:T(4,128)(2,1)S(1)} %get-tuple-element.6), channel_id=1, source_target_pairs={{0,1},{1,2},{2,3},{3,4},{4,5},{5,6},{6,7},{8,9},{9,10},{10,11},{11... | collective-permute-start | bytes 49160 | tf_op jit(solution)/shard_map/ppermute | solution.py:14
  31.5 8.0 %collective-permute-start.1 = (bf16[2,2,4,512]{3,2,1,0:T(4,128)(2,1)S(1)}, bf16[2,2,4,512]{3,2,1,0:T(4,128)(2,1)S(1)}, u32[]{:S(2)}, u32[]{:S(2)}) collective-permute-start(bf16[2,2,4,512]{3,2,1,0:T(4,128)(2,1)S(1)} %get-tuple-element.7), channel_id=1, source_target_pairs={{1,0},{2,1},{3,2},{4,3},{5,4},{6,5},{7,6},{9,8},{10,9},{11,10},{12... | collective-permute-start | bytes 49160 | tf_op jit(solution)/shard_map/ppermute | solution.py:17
  39.8 44.1 %collective-permute-start.2 = (bf16[2,2,264,512]{3,2,1,0:T(8,128)(2,1)S(1)}, bf16[2,2,264,512]{3,2,1,0:T(8,128)(2,1)S(1)}, u32[]{:S(2)}, u32[]{:S(2)}) collective-permute-start(bf16[2,2,264,512]{3,2,1,0:T(8,128)(2,1)S(1)} %pad_maximum_fusion), channel_id=1, source_target_pairs={{0,1},{1,0},{2,3},{3,2},{4,5},{5,4},{6,7},{7,6},{8,9},{9,8},{10,11... | collective-permute-start | bytes 3244040 | tf_op jit(solution)/shard_map/ppermute | solution.py:29
  83.8 97.1 %collective-permute-start.3 = (bf16[2,2,264,512]{3,2,1,0:T(8,128)(2,1)S(1)}, bf16[2,2,264,512]{3,2,1,0:T(8,128)(2,1)S(1)}, u32[]{:S(2)}, u32[]{:S(2)}) collective-permute-start(bf16[2,2,264,512]{3,2,1,0:T(8,128)(2,1)S(1)} %collective-permute-done.2), channel_id=1, source_target_pairs={{0,2},{2,0},{1,3},{3,1},{4,6},{6,4},{5,7},{7,5},{8,10},{10,8},{9,1... | collective-permute-start | bytes 3244040 | tf_op jit(solution)/shard_map/ppermute | solution.py:29
  180.9 27.8 %collective-permute-start.4 = (bf16[2,2,264,512]{3,2,1,0:T(8,128)(2,1)S(1)}, bf16[2,2,264,512]{3,2,1,0:T(8,128)(2,1)S(1)}, u32[]{:S(2)}, u32[]{:S(2)}) collective-permute-start(bf16[2,2,264,512]{3,2,1,0:T(8,128)(2,1)S(1)} %collective-permute-done.3), channel_id=1, source_target_pairs={{0,4},{4,0},{1,5},{5,1},{2,6},{6,2},{3,7},{7,3},{8,12},{12,8},{9,1... | collective-permute-start | bytes 3244040 | tf_op jit(solution)/shard_map/ppermute | solution.py:29
  247.6 3.7 copy-start
  257.1 26.9 %collective-permute-start.5 = (f32[2,256,512]{2,1,0:T(8,128)S(1)}, f32[2,256,512]{2,1,0:T(8,128)S(1)}, u32[]{:S(2)}, u32[]{:S(2)}) collective-permute-start(f32[2,256,512]{2,1,0:T(8,128)S(1)} %slice_bitcast_fusion), channel_id=1, source_target_pairs={{0,1},{1,0},{2,3},{3,2},{4,5},{5,4},{6,7},{7,6},{8,9},{9,8},{10,11... | collective-permute-start | bytes 3145736 | tf_op jit(solution)/shard_map/ppermute | solution.py:29
  284.0 32.5 %collective-permute-start.6 = (f32[2,256,512]{2,1,0:T(8,128)S(1)}, f32[2,256,512]{2,1,0:T(8,128)S(1)}, u32[]{:S(2)}, u32[]{:S(2)}) collective-permute-start(f32[2,256,512]{2,1,0:T(8,128)S(1)} %collective-permute-done.5), channel_id=1, source_target_pairs={{0,2},{2,0},{1,3},{3,1},{4,6},{6,4},{5,7},{7,5},{8,10},{10,8},{9,1... | collective-permute-start | bytes 3145736 | tf_op jit(solution)/shard_map/ppermute | solution.py:29
  316.5 280.0 %collective-permute-start.7 = (f32[2,256,512]{2,1,0:T(8,128)S(1)}, f32[2,256,512]{2,1,0:T(8,128)}, u32[]{:S(2)}, u32[]{:S(2)}) collective-permute-start(f32[2,256,512]{2,1,0:T(8,128)S(1)} %collective-permute-done.6), channel_id=1, source_target_pairs={{0,4},{4,0},{1,5},{5,1},{2,6},{6,2},{3,7},{7,3},{8,12},{12,8},{9,1... | collective-permute-start | bytes 3145736 | tf_op jit(solution)/shard_map/ppermute | solution.py:29
Sparse Core Ops, SparseCore 0:
  231.4 363.5 all-reduce.2
